TPU v7x, 128 devices: a whole 4x4x4 slice. The times are simulated.
128 devices in a mesh: row: 16 (over x, y_lo, core), col: 8 (over z, y_hi).
Axes of the slice: x: 4, y: 4 (y_hi: 2, y_lo: 2; y = y_hi * 2 + y_lo), z: 4, core: 2. Of those that a mesh axis runs over, the one named last changes fastest.
Arguments:
- orbitals: bfloat16 [12288, 6144], P('col', 'row'), may hold values from -6 to 6
- fock_blocks: bfloat16 [65536, 1024], P(('row', 'col')), may hold values from -0.078125 to 0.078125
- fock_where: int32 [65536], P(('row', 'col')), may hold values from 0 to 1151, as said below
- density_blocks: bfloat16 [5120, 1024], P(('row', 'col')), may hold values from -6 to 6
- integrals: bfloat16 [1024, 1024, 1024], P(('row', 'col')), may hold values from -0.1875 to 0.1875
- quartet_density: int32 [1024], P(('row', 'col')), may hold values from 0 to 5119, as said below
- quartet_target: int32 [1024], P(('row', 'col')), may hold values from 0 to 4095, as said below
- quartet_count: int32 [128], P(('row', 'col')), may hold values from 1 to 8, as said below
Outputs:
- applied_fock: bfloat16 [12288, 6144], P('row', 'col')
Inputs may be any that keep to these rules, and one draw needn't show every extreme that they name: `fock_where`: within one device the positions are distinct, from 0 to 1151. `quartet_density`: A quartet held by a device in row r names a density block held by a device in row r - 1, r or r + 1 (cyclically over 16 rows); device d holds blocks d * 40 to d * 40 + 39. `quartet_target`: the value t names block t % 512 of the device in column t // 512 of the quartet's own row. `quartet_count`: some device holds 8 live quartets; live quartets are the first slots of a device.
All inputs are finite; a program needn't handle non-finite values.
Results may differ from a plain program's by a relative error of at most 0.02.
Values may be sent and summed in bfloat16 or wider, within the bound.
No kernel may reach another device: no remote copies, remote signals or barrier semaphores. Data moves between devices by JAX's collectives and lax.ppermute only.
A program may use at most 320 MiB of HBM per device.

v0:
```python
import jax
import jax.numpy as jnp
from jax import lax
from jax.sharding import PartitionSpec as P

BS = 32
NA = 12288


def with_halo(shard, sides, width):
    for axis, dim in sides:
        size, length = (lax.axis_size(axis), shard.shape[dim])
        up = [(i, (i + 1) % size) for i in range(size)]
        down = [(j, i) for i, j in up]
        last = lax.slice_in_dim(shard, length - width, length, axis=dim)
        initial = lax.slice_in_dim(shard, 0, width, axis=dim)
        before = lax.ppermute(last, axis, up)
        after = lax.ppermute(initial, axis, down)
        shard = jnp.concatenate([before, shard, after], axis=dim)
    return shard


def body(
    orbitals,
    fock_blocks,
    fock_where,
    density_blocks,
    integrals,
    quartet_density,
    quartet_target,
    quartet_count,
):
    rows_axis = lax.axis_size("row")
    cols_axis = lax.axis_size("col")
    my_row = lax.axis_index("row")
    my_col = lax.axis_index("col")
    density_cap = density_blocks.shape[0]
    quartet_cap = integrals.shape[0]
    fock_cap = fock_blocks.shape[0]
    density_band = with_halo(density_blocks, (("row", 0),), density_cap)
    density_pool = lax.all_gather(density_band, "col", axis=0, tiled=True)
    per_row = cols_axis * density_cap
    source_row = quartet_density // per_row
    within = quartet_density % per_row
    offset = (source_row - my_row + 1 + rows_axis) % rows_axis
    picked = within // density_cap * (3 * density_cap) + offset * density_cap + within % density_cap
    vectors = jnp.take(density_pool, picked, axis=0)
    exchange_terms = jnp.einsum(
        "qij,qj->qi", integrals, vectors, preferred_element_type=jnp.float32
    )
    alive_mask = jnp.arange(quartet_cap, dtype=jnp.int32) < quartet_count[0]
    exchange_terms = jnp.where(alive_mask[:, None], exchange_terms, 0.0)
    slots_range = jnp.arange(fock_cap, dtype=jnp.int32)
    every_term, every_target = (
        lax.all_gather(exchange_terms.astype(jnp.bfloat16), "col", axis=0, tiled=True).astype(
            exchange_terms.dtype
        ),
        lax.all_gather(quartet_target, "col", axis=0, tiled=True),
    )
    is_mine = every_target // fock_cap == my_col
    chooser = jnp.logical_and(
        is_mine[None, :], (every_target % fock_cap)[None, :] == slots_range[:, None]
    )
    update = jnp.dot(chooser.astype(jnp.float32), every_term, precision=lax.Precision.HIGHEST)
    fock_new = (fock_blocks.astype(jnp.float32) + 0.25 * update).astype(jnp.bfloat16)
    tile_rows = NA // BS // rows_axis
    tile_cols = orbitals.shape[0] // BS
    tile_spots = jnp.arange(tile_rows * tile_cols, dtype=jnp.int32)
    placer = (fock_where[None, :] == tile_spots[:, None]).astype(jnp.bfloat16)
    dense_rows = jnp.dot(placer, fock_new, preferred_element_type=jnp.float32).astype(jnp.bfloat16)
    fock_tile = (
        dense_rows.reshape(tile_rows, tile_cols, BS, BS)
        .transpose(0, 2, 1, 3)
        .reshape(tile_rows * BS, tile_cols * BS)
    )
    partial_value = jnp.dot(
        fock_tile,
        lax.all_gather(orbitals, "row", axis=1, tiled=True),
        preferred_element_type=jnp.float32,
    ).astype(jnp.bfloat16)
    summed = lax.psum_scatter(partial_value, "col", scatter_dimension=1, tiled=True).astype(
        jnp.float32
    )
    return summed.astype(jnp.bfloat16)


def solution(mesh):
    return jax.shard_map(
        body,
        mesh=mesh,
        in_specs=(
            P("col", "row"),
            P(("row", "col"), None),
            P(("row", "col")),
            P(("row", "col"), None),
            P(("row", "col"), None, None),
            P(("row", "col")),
            P(("row", "col")),
            P(("row", "col")),
        ),
        out_specs=P("row", "col"),
        check_vma=False,
    )
```

profile of v0, /device:TPU:1, one launch (start us, length us, event | category | flops | bytes accessed | tf_op | source)
XLA Modules:
  0.0 325.0 jit_solution(17197109646016172554)
XLA Ops:
  6.5 0.0 all-gather.3.cloned.1.call-start
  6.5 2.7 collective-permute-start
  9.2 0.0 collective-permute-start.1
  9.2 1.8 collective-permute-done
  11.0 3.2 collective-permute-done.1
  14.2 1.6 pad_maximum_fusion
  15.8 0.0 all-gather.3.cloned.1.call-update
  15.8 0.0 all-gather.5.cloned.1.call-start
  15.8 0.7 all-gather.5.cloned.1.call-update
  16.6 0.0 reduce-scatter.2.cloned.1.call-start
  17.3 1.2 dynamic-slice
  19.1 0.9 dynamic-update-slice
  19.9 11.6 %all-reduce = s32[64]{0:T(128)S(1)} all-reduce(s32[64]{0:T(128)S(1)} %dynamic-update-slice), channel_id=1, replica_groups=mesh['row'=16,'col'=8] {'col'}, use_global_device_ids=true, to_apply=%add | all-reduce | flops 64 | bytes 512
  31.5 0.7 compare_and_fusion
  32.2 38.0 %all-gather.3.cloned.1.call-done = bf16[960,1024]{1,0:T(8,128)(2,1)} async-done(((bf16[120,1024]{1,0:T(8,128)(2,1)}), bf16[960,1024]{1,0:T(8,128)(2,1)}) %all-gather.3.cloned.1.call-update) | async-done | bytes 1966096 | tf_op jit(solution)/shard_map/all_gather | solution.py:41
  70.2 2.4 gather_fusion
  72.6 0.1 select_bitcast_fusion
  72.7 0.0 copy-start
  72.7 10.3 %fusion.6 = bf16[8,1,1024]{2,1,0:T(2,128)(2,1)S(1)} fusion(bf16[8,1024,1024]{2,1,0:T(8,128)(2,1)} %param.12, bf16[8,1024,1]{1,0,2:T(8,128)(2,1)S(1)} %select_bitcast_fusion), kind=kOutput, calls=%fused_computation.13 | convolution fusion | flops 16777216 | bytes 16809984 | tf_op jit(solution)/shard_map/qij,qj->qi/dot_general | solution.py:48
  82.9 0.0 copy-start.1
  82.9 0.1 fusion.5
  83.0 29.0 %all_gather.14 = bf16[64,1024]{1,0:T(8,128)(2,1)S(1)} all-gather(bf16[8,1024]{1,0:T(8,128)(2,1)S(1)} %fusion.5), channel_id=1, replica_groups=mesh['row'=16,'col'=8] {'col'}, dimensions={0}, use_global_device_ids=true | all-gather | bytes 147456 | tf_op jit(solution)/shard_map/all_gather | solution.py:55
  112.0 0.0 copy-done
  112.0 0.4 add_convert_fusion
  112.5 0.0 copy-done.1
  112.5 2.8 convolution_convert_fusion.1
  115.2 3.0 copy.9
  118.3 7.3 %reshape.18 = bf16[24,48,32,32]{1,0,3,2:T(8,128)(2,1)} reshape(bf16[1152,1024]{0,1:T(8,128)(2,1)S(1)} %copy.9) | data formatting | bytes 4718592 | tf_op jit(solution)/shard_map/reshape | solution.py:72
  125.6 11.5 %copy.10 = bf16[24,32,48,32]{3,2,1,0:T(8,128)(2,1)} copy(bf16[24,32,48,32]{2,0,3,1:T(8,128)(2,1)} %bitcast.19) | data formatting | bytes 4718592 | tf_op jit(solution)/shard_map/transpose | solution.py:73
  137.1 12.0 %reshape.19 = bf16[768,1536]{1,0:T(8,128)(2,1)S(1)} reshape(bf16[24,32,48,32]{3,2,1,0:T(8,128)(2,1)} %copy.10) | data formatting | bytes 4718592 | tf_op jit(solution)/shard_map/reshape | solution.py:74
  149.1 25.1 %all-gather.5.cloned.1.call-done = bf16[1536,6144]{1,0:T(8,128)(2,1)} async-done(((bf16[1536,384]{1,0:T(8,128)(2,1)}), bf16[1536,6144]{1,0:T(8,128)(2,1)}) %all-gather.5.cloned.1.call-update) | async-done | bytes 18874384 | tf_op jit(solution)/shard_map/all_gather | solution.py:78
  174.3 19.8 %convolution_convert_fusion = bf16[768,6144]{1,0:T(8,128)(2,1)} fusion(bf16[768,1536]{1,0:T(8,128)(2,1)S(1)} %reshape.19, bf16[1536,6144]{1,0:T(8,128)(2,1)} %all-gather.5.cloned.1.call-done), kind=kOutput, calls=%fused_computation.1 | convolution fusion | flops 14500233216 | bytes 30670848 | tf_op jit(solution)/shard_map/dot_general | solution.py:76
  194.0 0.0 reduce-scatter.2.cloned.1.call-update
  194.1 124.4 %reduce-scatter.2.cloned.1.call-done = bf16[768,768]{1,0:T(8,128)(2,1)} async-done(((bf16[768,6144]{1,0:T(8,128)(2,1)}), bf16[768,768]{1,0:T(8,128)(2,1)}) %reduce-scatter.2.cloned.1.call-update) | async-done | bytes 1179664 | tf_op jit(solution)/shard_map/reduce_scatter | solution.py:81
  (5 shorter events, 0.0 us)
Async XLA Ops:
  6.5 63.7 %all-gather.3.cloned.1.call-start = ((), (), s32[]{:S(2)}) async-start(), calls=%async_computation.1 | async-start | bytes 2211840 | tf_op jit(solution)/shard_map/all_gather | solution.py:41
  6.5 4.5 %collective-permute-start = (bf16[40,1024]{1,0:T(8,128)(2,1)}, bf16[40,1024]{1,0:T(8,128)(2,1)S(1)}, u32[]{:S(2)}, u32[]{:S(2)}) collective-permute-start(bf16[40,1024]{1,0:T(8,128)(2,1)} %param.11), channel_id=1, source_target_pairs={{0,8},{8,16},{16,24},{24,32},{32,40},{40,48},{48,56},{56,64},{64,7... | collective-permute-start | bytes 245768 | tf_op jit(solution)/shard_map/ppermute | solution.py:17
  9.2 5.0 %collective-permute-start.1 = (bf16[40,1024]{1,0:T(8,128)(2,1)}, bf16[40,1024]{1,0:T(8,128)(2,1)S(1)}, u32[]{:S(2)}, u32[]{:S(2)}) collective-permute-start(bf16[40,1024]{1,0:T(8,128)(2,1)} %param.11), channel_id=1, source_target_pairs={{8,0},{16,8},{24,16},{32,24},{40,32},{48,40},{56,48},{64,56},{72,6... | collective-permute-start | bytes 245768 | tf_op jit(solution)/shard_map/ppermute | solution.py:18
  15.8 158.5 %all-gather.5.cloned.1.call-start = ((), (), s32[]{:S(2)}) async-start(), calls=%async_computation.2 | async-start | bytes 20054016 | tf_op jit(solution)/shard_map/all_gather | solution.py:78
  16.6 301.9 %reduce-scatter.2.cloned.1.call-start = ((), (), s32[]{:S(2)}) async-start(), calls=%async_computation.3 | async-start | bytes 10616832 | tf_op jit(solution)/shard_map/reduce_scatter | solution.py:81
  72.7 39.4 %copy-start = (bf16[512,1024]{1,0:T(8,128)(2,1)S(1)}, bf16[512,1024]{1,0:T(8,128)(2,1)}, u32[]{:S(2)}) copy-start(bf16[512,1024]{1,0:T(8,128)(2,1)} %param.9) | copy-start | bytes 3145732
  82.9 29.5 %copy-start.1 = (s32[512]{0:T(512)S(1)}, s32[512]{0:T(512)}, u32[]{:S(2)}) copy-start(s32[512]{0:T(512)} %param.10) | copy-start | bytes 6148
Sparse Core Ops, SparseCore 0:
  15.9 54.2 all-gather.2
  71.9 102.3 all-gather.4
  194.2 124.2 reduce-scatter.1
where the time goes:
time: 326 us; the launch traced here: 325 us
  waiting for transfers between devices  193 us (59%)
  blocking collectives  40.5 us (12%)
  local copies, waits for them, and re-layouts  38.3 us (12%)
  matrix products  33.3 us (10%)
  between operations  14.4 us (4%)
    reduce_scatter x1, waiting for transfers between devices, body(): lax.psum_scatter(partial_value, 'col', scatter_dimension=1, tiled=True)  124 us
    all_gather x1, waiting for transfers between devices, body(): density_pool = lax.all_gather(density_band, 'col', axis=0, tiled=True)  38 us
    all_gather x1, blocking collectives, body(): lax.all_gather(exchange_terms.astype(jnp.bfloat16), 'col', axis=0, tiled=...  29 us
    all_gather x1, waiting for transfers between devices, body(): lax.all_gather(orbitals, 'row', axis=1, tiled=True)  25.1 us
    dot_general x1, matrix products, body(): jnp.dot(fock_tile, lax.all_gather(orbitals, 'row', axis=1, tiled=True), p...  19.8 us
    reshape x1, local copies, waits for them, and re-layouts, body(): fock_tile = dense_rows.reshape(tile_rows, tile_cols, BS, BS).transpose(0,...  12 us
    unnamed x1, blocking collectives  11.6 us
    transpose x1, local copies, waits for them, and re-layouts, body(): fock_tile = dense_rows.reshape(tile_rows, tile_cols, BS, BS).transpose(0,...  11.5 us
  transfers between devices with their start and end apart: 5, of which 5 were waited for; matrix products, arithmetic and copies ran while one was open for 16% of the time, Pallas kernels for 0%

commit v1 on v0

v1 whole, which is shorter than its diff:
```python
import functools

import jax
import jax.numpy as jnp
import numpy as np
from jax import lax
from jax.experimental import pallas as pl
from jax.experimental.pallas import tpu as pltpu
from jax.sharding import PartitionSpec as P

BS = 32
TROWS, TCOLS = 24, 48
KCAP, PCAP, QCAP = 512, 40, 8
ROWS, COLS = TROWS * BS, TCOLS * BS
GROUPS = TCOLS // 4
EXT = 1024 + 128
W = 128
AXES = ("row", "col")
MB = 1 << 20
bf16, f32 = jnp.bfloat16, jnp.float32


def coords(d):
    r, k = d // 8, d % 8
    return dict(x=r // 4, yl=r // 2 % 2, c=r % 2, z=k // 2, yh=k % 2)


def number(x, yl, c, z, yh):
    return ((x % 4) * 4 + yl * 2 + c) * 8 + (z % 4) * 2 + yh


def move(value, to):
    pairs = []
    for d in range(128):
        place = coords(d)
        target = dict(place)
        target.update(to(**place))
        pairs.append((d, number(**target)))
    return lax.ppermute(value, AXES, pairs)


def shift_x(value, by):
    return move(value, lambda x, **o: dict(x=x + by))


def shift_z(value, by):
    return move(value, lambda z, **o: dict(z=z + by))


def swap_core(value):
    return move(value, lambda c, **o: dict(c=1 - c))


def swap_yh(value):
    return move(value, lambda yh, **o: dict(yh=1 - yh))


def shift_row(value, by):
    pairs = [(d, (d + 8 * by) % 128) for d in range(128)]
    return lax.ppermute(value, AXES, pairs)


def move_y(value, table):
    def to(yl, yh, **o):
        y = table[yh * 2 + yl]
        return dict(yl=y % 2, yh=y // 2)

    return move(value, to)


def here():
    r, k = lax.axis_index("row"), lax.axis_index("col")
    return dict(r=r, k=k, x=r // 4, yl=r // 2 % 2, c=r % 2, z=k // 2, yh=k % 2)


def call(kernel, out_shape, flops, nbytes, **kw):
    return pl.pallas_call(
        kernel,
        out_shape=out_shape,
        compiler_params=pltpu.CompilerParams(vmem_limit_bytes=56 * MB),
        cost_estimate=pl.CostEstimate(flops=flops, bytes_accessed=nbytes, transcendentals=0),
        **kw,
    )


VM = pl.BlockSpec(memory_space=pltpu.VMEM)
SM = pl.BlockSpec(memory_space=pltpu.SMEM)
ANY = pl.BlockSpec(memory_space=pl.ANY)


def select_kernel(req_own, req_a, req_b, p0, p1, p2, p3, out_own, out_a, out_b):
    at = here()
    parts = (p0, p1, p2, p3)
    steps = (0, 3, 1, 2)
    span = 2 * PCAP
    lane = lax.broadcasted_iota(jnp.int32, (16, span), 1)
    row = lax.broadcasted_iota(jnp.int32, (16, span), 0)
    for req, out in ((req_own, out_own), (req_a, out_a), (req_b, out_b)):
        want = jnp.full((16, span), -1, jnp.int32)
        for q in range(QCAP):
            want = jnp.where(row == q, req[q], want)
        total = jnp.zeros((16, 1024), f32)
        for part, step in zip(parts, steps):
            z = (at["z"] + step) % 4
            yh = jnp.where(lane < PCAP, at["yh"], 1 - at["yh"])
            held = (at["r"] * 8 + z * 2 + yh) * PCAP + jnp.where(lane < PCAP, lane, lane - PCAP)
            hot = (want == held).astype(f32).astype(bf16)
            total = total + jnp.dot(hot, part[...], preferred_element_type=f32)
        out[...] = total.astype(bf16)


def select(requests, parts):
    shape = jax.ShapeDtypeStruct((16, 1024), bf16)
    return call(
        select_kernel,
        (shape,) * 3,
        48 * 320 * 2048,
        320 * 2048 * 4,
        in_specs=[SM] * 3 + [VM] * 4,
        out_specs=[VM] * 3,
    )(*requests, *parts)


def terms_kernel(count, target, v0, v1, v2, integral, out, acc, vt):
    q = pl.program_id(0)

    @pl.when(q == 0)
    def _():
        v = v0[...].astype(f32) + v1[...].astype(f32) + v2[...].astype(f32)
        vt[:, 0:16] = v.T
        vt[:, 16:128] = jnp.zeros((1024, 112), f32)
        acc[...] = jnp.zeros_like(acc)

    lane = lax.broadcasted_iota(jnp.int32, (1024, 128), 1)
    live = q < count[0]
    side = jnp.where(jnp.logical_and(lane == q, live), vt[...], 0.0).astype(bf16)
    acc[...] += jnp.dot(integral[0], side, preferred_element_type=f32)

    @pl.when(q == QCAP - 1)
    def _():
        out[:, 0:1024] = acc[...].T[0:QCAP, :].astype(bf16)
        col = lax.broadcasted_iota(jnp.int32, (QCAP, 128), 1)
        row = lax.broadcasted_iota(jnp.int32, (QCAP, 128), 0)
        mark = jnp.zeros((QCAP, 128), jnp.int32)
        for i in range(QCAP):
            t = target[i]
            note = jnp.where(col == 0, t // KCAP, jnp.where(col == 1, t % KCAP // 32, jnp.where(col == 2, t % 32, 0)))
            mark = jnp.where(row == i, note, mark)
        out[:, 1024:EXT] = mark.astype(f32).astype(bf16)


def exchange(count, target, vectors, integrals):
    return call(
        terms_kernel,
        jax.ShapeDtypeStruct((QCAP, EXT), bf16),
        QCAP * 2 * 1024 * 1024 * 128,
        QCAP * 2 * MB,
        grid=(QCAP,),
        in_specs=[SM, SM, VM, VM, VM, pl.BlockSpec((1, 1024, 1024), lambda q: (q, 0, 0))],
        out_specs=pl.BlockSpec((QCAP, EXT), lambda q: (0, 0)),
        scratch_shapes=[pltpu.VMEM((1024, 128), f32), pltpu.VMEM((1024, 128), f32)],
    )(count, target, *vectors, integrals)


def tiles_kernel(where, f0, f1, f2, f3, t0, t1, t2, t3, t4, out, fcur, tcur, wide, spread):
    g = pl.program_id(0)
    at = here()
    for i, f in enumerate((f0, f1, f2, f3)):

        @pl.when(g == i)
        def _():
            fcur[...] = f[...]

    @pl.when(g == 0)
    def _():
        for i, t in enumerate((t0, t1, t2, t3)):
            tcur[16 * i : 16 * i + 16, :] = t[...]

    @pl.when(g == 2)
    def _():
        tcur[...] = t4[...]

    k = at["z"] * 2 + jnp.where(g % 2 == 0, at["yh"], 1 - at["yh"])
    marks = tcur[:, 1024:EXT].astype(f32)
    slot = (marks[:, 1:2] * 32.0 + marks[:, 2:3]).astype(jnp.int32)
    slot = jnp.where(marks[:, 0:1].astype(jnp.int32) == k, slot, -1)
    spots = lax.broadcasted_iota(jnp.int32, (64, KCAP), 1)
    hot = (slot == spots).astype(f32).astype(bf16)
    update = lax.dot_general(hot, tcur[:, 0:1024], (((0,), (0,)), ((), ())), preferred_element_type=f32)
    fock = (fcur[:, 0:1024].astype(f32) + 0.25 * update).astype(bf16)
    place = fcur[:, 1024:EXT].astype(f32)
    tr = place[:, 0:1].astype(jnp.int32)
    tc = place[:, 1:2].astype(jnp.int32)
    lane = lax.broadcasted_iota(jnp.int32, (KCAP, 512), 1)
    keep = (lane % 128 // BS) == (tc % 4)
    src = lax.broadcasted_iota(jnp.int32, (128, 512), 0)
    dst = lax.broadcasted_iota(jnp.int32, (128, 512), 1)
    copy = (src == dst // 128 * BS + dst % BS).astype(f32).astype(bf16)
    for a in range(8):
        piece = jnp.dot(fock[:, a * 128 : (a + 1) * 128], copy, preferred_element_type=f32)
        wide[:, a * 512 : (a + 1) * 512] = jnp.where(keep, piece, 0.0).astype(bf16)
    spot = lax.broadcasted_iota(jnp.int32, (KCAP, GROUPS * TROWS), 1)
    put = (spot == tc // 4 * TROWS + tr).astype(f32).astype(bf16)
    for h in range(8):
        spread[...] = lax.dot_general(
            put, wide[:, h * 512 : (h + 1) * 512], (((0,), (0,)), ((), ())), preferred_element_type=f32
        )
        for p in range(2):
            for t in range(GROUPS):
                pair = [
                    spread[t * TROWS : (t + 1) * TROWS, (2 * p + o) * 128 : (2 * p + o + 1) * 128]
                    for o in range(2)
                ]
                start = (4 * h + 2 * p) * TROWS
                out[start : start + 2 * TROWS, t * 128 : (t + 1) * 128] = jnp.concatenate(pair, axis=0).astype(bf16)


def tiles(focks, terms, places):
    spec = pltpu.PrefetchScalarGridSpec(
        num_scalar_prefetch=1,
        grid=(4,),
        in_specs=[VM] * 9,
        out_specs=pl.BlockSpec((ROWS, COLS), lambda g, w: (w[2 * g], w[2 * g + 1])),
        scratch_shapes=[
            pltpu.VMEM((KCAP, EXT), bf16),
            pltpu.VMEM((64, EXT), bf16),
            pltpu.VMEM((KCAP, 4096), bf16),
            pltpu.VMEM((GROUPS * TROWS, 512), f32),
        ],
    )
    return call(
        tiles_kernel,
        jax.ShapeDtypeStruct((2 * ROWS, 2 * COLS), bf16),
        10 * 10**9,
        16 * MB,
        grid_spec=spec,
    )(places, *focks, *terms)


def product_kernel(mat, own, left, right, far_a, far_b, p2t, p2b, pp, pm, p0, cols, sems):
    i = pl.program_id(0)
    at = here()

    @pl.when(i == 0)
    def _():
        copies = []
        plan = ((own, 0, 0, 2), (left, 3, 0, 2), (right, 1, 0, 2), (far_a, 2, 0, 1), (far_b, 2, 1, 1))
        for n, (ref, step, first, halves) in enumerate(plan):
            lane = pl.multiple_of((at["x"] + step - at["z"] + 4) % 4 * W, W)
            dst = cols.at[first * COLS : (first + halves) * COLS, pl.ds(lane, W)]
            copy = pltpu.make_async_copy(ref, dst, sems.at[n])
            copy.start()
            copies.append(copy)
        for copy in copies:
            copy.wait()

    full = jnp.dot(mat[...], cols[...], preferred_element_type=f32)
    p0[...] = full[:, 0:W].astype(bf16)
    pp[...] = full[:, W : 2 * W].astype(bf16)
    pm[...] = full[:, 3 * W : 4 * W].astype(bf16)

    @pl.when(i == 0)
    def _():
        p2t[...] = full[:, 2 * W : 3 * W].astype(bf16)

    @pl.when(i == 1)
    def _():
        p2b[...] = full[:, 2 * W : 3 * W].astype(bf16)


def product(mat, blocks):
    half = jax.ShapeDtypeStruct((ROWS, W), bf16)
    both = jax.ShapeDtypeStruct((2 * ROWS, W), bf16)
    fixed = pl.BlockSpec((ROWS, W), lambda i: (0, 0))
    moving = pl.BlockSpec((ROWS, W), lambda i: (i, 0))
    return call(
        product_kernel,
        (half, half, both, both, both),
        2 * 1536 * 3072 * 512,
        14 * MB,
        grid=(2,),
        in_specs=[pl.BlockSpec((ROWS, 2 * COLS), lambda i: (i, 0))] + [ANY] * 5,
        out_specs=[fixed, fixed, moving, moving, moving],
        scratch_shapes=[pltpu.VMEM((2 * COLS, 4 * W), bf16), pltpu.SemaphoreType.DMA((5,))],
    )(mat, *blocks)


def finish_kernel(k0, k1, k2, g0, g1, g2, out, joined):
    c = lax.axis_index("row") % 2
    mine = pl.multiple_of(c * (3 * W), W)
    other = pl.multiple_of((1 - c) * (3 * W), W)
    for j, (a, b) in enumerate(((k0, g0), (k1, g1), (k2, g2))):
        joined[:, pl.ds(mine + j * W, W)] = a[...]
        joined[:, pl.ds(other + j * W, W)] = b[...]
    row = lax.broadcasted_iota(jnp.int32, (ROWS, ROWS), 0)
    col = lax.broadcasted_iota(jnp.int32, (ROWS, ROWS), 1)
    order = (col == row % BS * TROWS + row // BS).astype(f32).astype(bf16)
    out[...] = jnp.dot(order, joined[...], preferred_element_type=f32).astype(bf16)


def finish(kept, got):
    return call(
        finish_kernel,
        jax.ShapeDtypeStruct((ROWS, 6 * W), bf16),
        2 * ROWS**3,
        4 * MB,
        in_specs=[VM] * 6,
        out_specs=VM,
        scratch_shapes=[pltpu.VMEM((ROWS, 6 * W), bf16)],
    )(*kept, *got)


def body(
    orbitals,
    fock_blocks,
    fock_where,
    density_blocks,
    integrals,
    quartet_density,
    quartet_target,
    quartet_count,
):
    at = here()
    with jax.named_scope("density"):
        ask_above = shift_row(quartet_density, -1)
        ask_below = shift_row(quartet_density, 1)
        pair = jnp.concatenate([density_blocks, swap_yh(density_blocks)], axis=0)
        pool = (pair, shift_z(pair, 1), shift_z(pair, -1), shift_z(pair, 2))
        own, for_above, for_below = select((quartet_density, ask_above, ask_below), pool)
        vectors = (own, shift_row(for_above, 1), shift_row(for_below, -1))
    with jax.named_scope("terms"):
        term = exchange(quartet_count, quartet_target, vectors, integrals)
        term2 = jnp.concatenate([term, swap_yh(term)], axis=0)
        row_terms = (term2, shift_z(term2, 1), shift_z(term2, -1), shift_z(term2, 2))
        other_terms = swap_core(jnp.concatenate(row_terms, axis=0))
    with jax.named_scope("fock"):
        spot = jnp.stack([fock_where // TCOLS, fock_where % TCOLS], axis=1).astype(bf16)
        fock = jnp.concatenate([fock_blocks, jnp.pad(spot, ((0, 0), (0, 126)))], axis=1)
        fock_h = swap_yh(fock)
        fock_c = swap_core(fock)
        fock_hc = swap_core(fock_h)
        own_slot = jnp.where(at["yh"] == at["yl"], 1, 0)
        c = at["c"]
        places = jnp.stack([c, own_slot, c, 1 - own_slot, 1 - c, own_slot, 1 - c, 1 - own_slot]).astype(jnp.int32)
        mat = tiles((fock, fock_h, fock_c, fock_hc), (*row_terms, other_terms), places)
    blocks = []
    for j in range(3):
        with jax.named_scope("gather"):
            piece = orbitals[:, j * W : (j + 1) * W]
            slots = jnp.concatenate([move_y(piece, (1, 3, 0, 2)), move_y(piece, (0, 2, 1, 3))], axis=0)
            left, right = shift_x(slots, 1), shift_x(slots, -1)
            far_a = shift_x(left[:COLS], 1)
            far_b = shift_x(right[COLS:], -1)
            blocks.append((slots, left, right, far_a, far_b))
    kept, got = [], []
    for j in range(3):
        with jax.named_scope("reduce"):
            p2t, p2b, pp, pm, p0 = product(mat, blocks[j])
            from_below = shift_z(p2t, 1)
            from_above = shift_z(p2b, -1)
            pp = jnp.concatenate([(pp[:ROWS].astype(f32) + from_below.astype(f32)).astype(bf16), pp[ROWS:]], axis=0)
            pm = jnp.concatenate([pm[:ROWS], (pm[ROWS:].astype(f32) + from_above.astype(f32)).astype(bf16)], axis=0)
            a, b = shift_z(pp, 1), shift_z(pm, -1)
            total = (p0.astype(f32) + a.astype(f32) + b.astype(f32)).astype(bf16).reshape(2, ROWS, W)
            kept.append(lax.dynamic_index_in_dim(total, c, 0, keepdims=False))
            got.append(swap_core(lax.dynamic_index_in_dim(total, 1 - c, 0, keepdims=False)))
    with jax.named_scope("finish"):
        return finish(kept, got)


def solution(mesh):
    return jax.shard_map(
        body,
        mesh=mesh,
        in_specs=(
            P("col", "row"),
            P(("row", "col"), None),
            P(("row", "col")),
            P(("row", "col"), None),
            P(("row", "col"), None, None),
            P(("row", "col")),
            P(("row", "col")),
            P(("row", "col")),
        ),
        out_specs=P("row", "col"),
        check_vma=False,
    )
```

time: 326 us -> 244 us (0.75)
  waiting for transfers between devices: 193 us -> 63.1 us
  starting transfers between devices: 2.77 us -> 86.4 us
  Pallas kernels: 0 us -> 68.4 us
  blocking collectives: 40.5 us -> 0 us
  matrix products: 33.3 us -> 0 us
  local copies, waits for them, and re-layouts: 38.3 us -> 23 us
  between operations: 14.4 us -> 1.44 us
    reduce_scatter x1 -> x0, waiting for transfers between devices: 124 us -> none  [body(): lax.psum_scatter(partial_value, 'col', scatter_dimension=1, tiled=True)]
    ppermute x2 -> x49, starting transfers between devices: 2.69 us -> 86.4 us  [the longest x45 80 us: move(): return lax.ppermute(value, AXES, pairs)]
    pallas_call x0 -> x7, Pallas kernels: none -> 68.4 us  [the longest x3 33.3 us: product(): call(product_kernel, (half, half, both, both, both), 2 * 1536 * 3072 * 51...]
    all_gather x2 -> x0, waiting for transfers between devices: 63.1 us -> none  [the longest x1 38 us: body(): density_pool = lax.all_gather(density_band, 'col', axis=0, tiled=True)]
    ppermute x2 -> x49, waiting for transfers between devices: 4.95 us -> 63.1 us  [the longest x45 54.6 us: move(): return lax.ppermute(value, AXES, pairs)]
    dot_general x4 -> x0, matrix products: 33.3 us -> none  [the longest x1 19.8 us: body(): jnp.dot(fock_tile, lax.all_gather(orbitals, 'row', axis=1, tiled=True), p...]
    all_gather x1 -> x0, blocking collectives: 29 us -> none  [body(): lax.all_gather(exchange_terms.astype(jnp.bfloat16), 'col', axis=0, tiled=...]
    reshape x2 -> x0, local copies, waits for them, and re-layouts: 19.3 us -> none  [the longest x1 12 us: body(): fock_tile = dense_rows.reshape(tile_rows, tile_cols, BS, BS).transpose(0,...]
  transfers between devices with their start and end apart: 5 -> 49, of which waited for: 5 -> 12; matrix products, arithmetic and copies ran while one was open for 16% -> 8% of each run, Pallas kernels for 0% -> 27%
where the time goes in v1:
time: 244 us; the launch traced here: 243 us
  starting transfers between devices  86.4 us (35%)
  Pallas kernels  68.4 us (28%)
  waiting for transfers between devices  63.1 us (26%)
  local copies, waits for them, and re-layouts  23 us (9%)
    ppermute x45, starting transfers between devices, move(): return lax.ppermute(value, AXES, pairs)  80 us
    ppermute x45, waiting for transfers between devices, move(): return lax.ppermute(value, AXES, pairs)  54.6 us
    pallas_call x3, Pallas kernels, product(): call(product_kernel, (half, half, both, both, both), 2 * 1536 * 3072 * 51...  33.3 us
    pallas_call x1, Pallas kernels, tiles(): call(tiles_kernel, jax.ShapeDtypeStruct((2 * ROWS, 2 * COLS), bf16), 10 *...  17.6 us
    pallas_call x1, Pallas kernels, exchange(): call(terms_kernel, jax.ShapeDtypeStruct((QCAP, EXT), bf16), QCAP * 2 * 10...  11.6 us
    unnamed x92, local copies, waits for them, and re-layouts  9.22 us
    ppermute x4, waiting for transfers between devices, shift_row(): return lax.ppermute(value, AXES, pairs)  8.53 us
    ppermute x4, starting transfers between devices, shift_row(): return lax.ppermute(value, AXES, pairs)  6.39 us
  transfers between devices with their start and end apart: 49, of which 12 were waited for; matrix products, arithmetic and copies ran while one was open for 8% of the time, Pallas kernels for 27%

profile of v1, /device:TPU:1, one launch (start us, length us, event | category | flops | bytes accessed | tf_op | source)
XLA Modules:
  0.0 243.4 jit_solution(16274818527682287230)
XLA Ops:
  0.0 1.4 collective-permute-start.3
  1.4 1.3 collective-permute-start.4
  2.8 2.7 %collective-permute-start.5 = (bf16[40,1024]{1,0:T(8,128)(2,1)}, bf16[40,1024]{1,0:T(8,128)(2,1)S(1)}, u32[]{:S(2)}, u32[]{:S(2)}) collective-permute-start(bf16[40,1024]{1,0:T(8,128)(2,1)} %param.11), channel_id=1, source_target_pairs={{0,1},{1,0},{2,3},{3,2},{4,5},{5,4},{6,7},{7,6},{8,9},{9,8},{10,11... | collective-permute-start | bytes 245768 | tf_op jit(solution)/shard_map/density/ppermute | solution.py:39
  5.5 1.3 fusion.5
  6.8 1.0 collective-permute-done.5
  7.8 1.7 collective-permute-start.6
  9.5 2.2 collective-permute-start.7
  11.7 1.2 collective-permute-start.8
  13.0 2.1 collective-permute-start.36
  15.8 3.3 %collective-permute-start.26 = (bf16[1536,128]{1,0:T(8,128)(2,1)S(1)}, bf16[1536,128]{1,0:T(8,128)(2,1)}, u32[]{:S(2)}, u32[]{:S(2)}) collective-permute-start(bf16[1536,128]{1,0:T(8,128)(2,1)S(1)} %get-tuple-element.43), channel_id=1, source_target_pairs={{0,16},{1,0},{2,18},{3,2},{4,20},{5,4},{6,22},{7,6},{8,24},{9,8},{... | collective-permute-start | bytes 1179656 | tf_op jit(solution)/shard_map/gather/ppermute | solution.py:39
  20.4 2.2 density.1
  22.6 3.4 %collective-permute-start.10 = (bf16[16,1024]{1,0:T(8,128)(2,1)}, bf16[16,1024]{1,0:T(8,128)(2,1)S(1)}, u32[]{:S(2)}, u32[]{:S(2)}) collective-permute-start(bf16[16,1024]{1,0:T(8,128)(2,1)} %get-tuple-element.25), channel_id=1, source_target_pairs={{0,120},{1,121},{2,122},{3,123},{4,124},{5,125},{6,126},{7,127},{8... | collective-permute-start | bytes 98312 | tf_op jit(solution)/shard_map/density/ppermute | solution.py:60
  27.1 8.5 %collective-permute-done.10.v2 = bf16[16,1024]{1,0:T(8,128)(2,1)S(1)} collective-permute-done((bf16[16,1024]{1,0:T(8,128)(2,1)}, bf16[16,1024]{1,0:T(8,128)(2,1)S(1)}, u32[]{:S(2)}, u32[]{:S(2)}) %collective-permute-start.10) | collective-permute-done | bytes 32800 | tf_op jit(solution)/shard_map/density/ppermute | solution.py:60
  36.9 11.6 %terms.1 = bf16[8,1152]{1,0:T(8,128)(2,1)} custom-call(s32[1]{0:T(128)S(6)} %copy.20.count, s32[8]{0:T(128)} %target.1, bf16[16,1024]{1,0:T(8,128)(2,1)} %get-tuple-element.23.v0, bf16[16,1024]{1,0:T(8,128)(2,1)} %copy-done.28, bf16[16,1024]{1,0:T(8,128)(2,1)} %copy-done.27, bf16[8,1024,1024]{2,1,0:T(8,128)(2,1)} %integral.1), custom_call_target="tpu_custom_call" | custom-call | flops 2147483648 | bytes 16777216 | tf_op jit(solution)/shard_map/terms/pallas_call | solution.py:153
  48.5 1.8 collective-permute-start.11
  50.4 2.4 collective-permute-done.11
  52.8 1.8 collective-permute-start
  54.9 0.8 collective-permute-start.12
  55.7 1.0 constant_dynamic-update-slice_fusion.10
  56.8 2.0 collective-permute-start.13
  59.5 1.8 collective-permute-start.38
  62.1 2.0 collective-permute-done.14.t3
  64.1 3.7 %collective-permute-start.39 = (bf16[3072,128]{1,0:T(8,128)(2,1)S(1)}, bf16[3072,128]{1,0:T(8,128)(2,1)S(1)}, u32[]{:S(2)}, u32[]{:S(2)}) collective-permute-start(bf16[3072,128]{1,0:T(8,128)(2,1)S(1)} %constant_dynamic-update-slice_fusion.11.own), channel_id=1, source_target_pairs={{0,96},{1,97},{2,98},{3,99},{4,100},{5,101},{6,102},{7,103},{8,104... | collective-permute-start | bytes 2359304 | tf_op jit(solution)/shard_map/gather/ppermute | solution.py:39
  67.8 21.0 %collective-permute-done.16 = bf16[1536,128]{1,0:T(8,128)(2,1)S(1)} collective-permute-done((bf16[1536,128]{1,0:T(8,128)(2,1)S(1)}, bf16[1536,128]{1,0:T(8,128)(2,1)S(1)}, u32[]{:S(2)}, u32[]{:S(2)}) %collective-permute-start.16) | collective-permute-done | bytes 393248 | tf_op jit(solution)/shard_map/gather/ppermute | solution.py:39
  88.9 1.9 collective-permute-start.28
  92.0 2.2 collective-permute-start.1
  94.3 0.8 constant_dynamic-update-slice_fusion.8
  95.0 1.6 collective-permute-start.29
  96.7 0.8 constant_dynamic-update-slice_fusion.7.own
  97.5 10.4 %collective-permute-done.28.left = bf16[3072,128]{1,0:T(8,128)(2,1)S(1)} collective-permute-done((bf16[3072,128]{1,0:T(8,128)(2,1)S(1)}, bf16[3072,128]{1,0:T(8,128)(2,1)S(1)}, u32[]{:S(2)}, u32[]{:S(2)}) %collective-permute-start.28) | collective-permute-done | bytes 786464 | tf_op jit(solution)/shard_map/gather/ppermute | solution.py:39
  108.0 1.3 collective-permute-start.19
  111.1 2.7 %collective-permute-done.29.right = bf16[3072,128]{1,0:T(8,128)(2,1)} collective-permute-done((bf16[3072,128]{1,0:T(8,128)(2,1)S(1)}, bf16[3072,128]{1,0:T(8,128)(2,1)}, u32[]{:S(2)}, u32[]{:S(2)}) %collective-permute-start.29) | collective-permute-done | bytes 786464 | tf_op jit(solution)/shard_map/gather/ppermute | solution.py:39
  113.8 3.4 %collective-permute-start.15 = (bf16[64,1152]{1,0:T(8,128)(2,1)}, bf16[64,1152]{1,0:T(8,128)(2,1)}, u32[]{:S(2)}, u32[]{:S(2)}) collective-permute-start(bf16[64,1152]{1,0:T(8,128)(2,1)} %constant_dynamic-update-slice_fusion.2), channel_id=1, source_target_pairs={{0,8},{1,9},{2,10},{3,11},{4,12},{5,13},{6,14},{7,15},{8,0},{9,1},... | collective-permute-start | bytes 442376 | tf_op jit(solution)/shard_map/terms/ppermute | solution.py:39
  118.0 1.0 slice.87
  119.0 5.9 %collective-permute-done.18.left = bf16[3072,128]{1,0:T(8,128)(2,1)} collective-permute-done((bf16[3072,128]{1,0:T(8,128)(2,1)}, bf16[3072,128]{1,0:T(8,128)(2,1)}, u32[]{:S(2)}, u32[]{:S(2)}) %collective-permute-start.18) | collective-permute-done | bytes 786464 | tf_op jit(solution)/shard_map/gather/ppermute | solution.py:39
  124.9 1.0 slice.84
  125.9 3.4 %collective-permute-done.19.right = bf16[3072,128]{1,0:T(8,128)(2,1)} collective-permute-done((bf16[3072,128]{1,0:T(8,128)(2,1)}, bf16[3072,128]{1,0:T(8,128)(2,1)}, u32[]{:S(2)}, u32[]{:S(2)}) %collective-permute-start.19) | collective-permute-done | bytes 786464 | tf_op jit(solution)/shard_map/gather/ppermute | solution.py:39
  129.4 2.8 %collective-permute-start.41 = (bf16[1536,128]{1,0:T(8,128)(2,1)S(1)}, bf16[1536,128]{1,0:T(8,128)(2,1)S(1)}, u32[]{:S(2)}, u32[]{:S(2)}) collective-permute-start(bf16[1536,128]{1,0:T(8,128)(2,1)S(1)} %slice.89), channel_id=1, source_target_pairs={{0,96},{1,97},{2,98},{3,99},{4,100},{5,101},{6,102},{7,103},{8,104... | collective-permute-start | bytes 1179656 | tf_op jit(solution)/shard_map/gather/ppermute | solution.py:39
  132.1 1.0 slice.85
  133.3 2.7 %collective-permute-start.31 = (bf16[1536,128]{1,0:T(8,128)(2,1)S(1)}, bf16[1536,128]{1,0:T(8,128)(2,1)S(1)}, u32[]{:S(2)}, u32[]{:S(2)}) collective-permute-start(bf16[1536,128]{1,0:T(8,128)(2,1)S(1)} %slice.87), channel_id=1, source_target_pairs={{0,96},{1,97},{2,98},{3,99},{4,100},{5,101},{6,102},{7,103},{8,104... | collective-permute-start | bytes 1179656 | tf_op jit(solution)/shard_map/gather/ppermute | solution.py:39
  135.9 17.6 %fock.1.mat = bf16[1536,3072]{1,0:T(8,128)(2,1)} custom-call(s32[8]{0:T(128)} %stack.35.where, bf16[512,1152]{1,0:T(8,128)(2,1)} %copy-done, bf16[512,1152]{1,0:T(8,128)(2,1)} %collective-permute-done.f1, bf16[512,1152]{1,0:T(8,128)(2,1)} %collective-permute-done.1.f2, bf16[512,1152]{1,0:T(8,128)(2,1)} %collective-permute-done.2.f3, ...), custom_call_target="tpu_custom_call" | custom-call | flops 10000000000 | bytes 16777216 | tf_op jit(solution)/shard_map/fock/pallas_call | solution.py:231
  153.6 2.7 %collective-permute-start.21 = (bf16[1536,128]{1,0:T(8,128)(2,1)S(1)}, bf16[1536,128]{1,0:T(8,128)(2,1)S(1)}, u32[]{:S(2)}, u32[]{:S(2)}) collective-permute-start(bf16[1536,128]{1,0:T(8,128)(2,1)S(1)} %slice.85), channel_id=1, source_target_pairs={{0,96},{1,97},{2,98},{3,99},{4,100},{5,101},{6,102},{7,103},{8,104... | collective-permute-start | bytes 1179656 | tf_op jit(solution)/shard_map/gather/ppermute | solution.py:39
  157.0 11.1 %reduce.5 = (bf16[768,128]{1,0:T(8,128)(2,1)}, bf16[768,128]{1,0:T(8,128)(2,1)}, bf16[1536,128]{1,0:T(8,128)(2,1)}, bf16[1536,128]{1,0:T(8,128)(2,1)}, bf16[1536,128]{1,0:T(8,128)(2,1)}) custom-call(bf16[1536,3072]{1,0:T(8,128)(2,1)} %fock.1.mat, bf16[3072,128]{1,0:T(8,128)(2,1)} %copy-done.17, bf16[3072,128]{1,0:T(8,128)(2,1)} %copy-done.13, ...), custom_call_target="tpu_custom_call" | custom-call | flops 4831838208 | bytes 14680064 | tf_op jit(solution)/shard_map/reduce/pallas_call | solution.py:276
  168.1 0.8 collective-permute-start.42
  168.9 0.9 slice.81
  169.9 0.9 slice.82
  170.8 2.0 collective-permute-start.44
  172.9 0.8 copy-done.35
  173.6 11.2 %reduce.4 = (bf16[768,128]{1,0:T(8,128)(2,1)}, bf16[768,128]{1,0:T(8,128)(2,1)}, bf16[1536,128]{1,0:T(8,128)(2,1)}, bf16[1536,128]{1,0:T(8,128)(2,1)}, bf16[1536,128]{1,0:T(8,128)(2,1)}) custom-call(bf16[1536,3072]{1,0:T(8,128)(2,1)} %fock.1.mat, bf16[3072,128]{1,0:T(8,128)(2,1)} %copy-done.16, bf16[3072,128]{1,0:T(8,128)(2,1)} %copy-done.12, ...), custom_call_target="tpu_custom_call" | custom-call | flops 4831838208 | bytes 14680064 | tf_op jit(solution)/shard_map/reduce/pallas_call | solution.py:276
  184.9 0.9 slice.74
  185.8 2.7 %collective-permute-start.34 = (bf16[768,128]{1,0:T(8,128)(2,1)}, bf16[768,128]{1,0:T(8,128)(2,1)S(1)}, u32[]{:S(2)}, u32[]{:S(2)}) collective-permute-start(bf16[768,128]{1,0:T(8,128)(2,1)} %get-tuple-element.35), channel_id=1, source_target_pairs={{0,6},{1,7},{2,0},{3,1},{4,2},{5,3},{6,4},{7,5},{8,14},{9,15},{10,... | collective-permute-start | bytes 589832 | tf_op jit(solution)/shard_map/reduce/ppermute | solution.py:39
  188.6 0.8 copy-done.34
  189.3 11.1 %reduce.3 = (bf16[768,128]{1,0:T(8,128)(2,1)}, bf16[768,128]{1,0:T(8,128)(2,1)}, bf16[1536,128]{1,0:T(8,128)(2,1)}, bf16[1536,128]{1,0:T(8,128)(2,1)}, bf16[1536,128]{1,0:T(8,128)(2,1)}) custom-call(bf16[1536,3072]{1,0:T(8,128)(2,1)} %fock.1.mat, bf16[3072,128]{1,0:T(8,128)(2,1)} %constant_dynamic-update-slice_fusion.7.own, ...), custom_call_target="tpu_custom_call" | custom-call | flops 4831838208 | bytes 14680064 | tf_op jit(solution)/shard_map/reduce/pallas_call | solution.py:276
  200.5 1.0 slice.67
  201.6 0.9 slice.68
  202.6 2.6 %collective-permute-start.24 = (bf16[768,128]{1,0:T(8,128)(2,1)S(1)}, bf16[768,128]{1,0:T(8,128)(2,1)S(1)}, u32[]{:S(2)}, u32[]{:S(2)}) collective-permute-start(bf16[768,128]{1,0:T(8,128)(2,1)S(1)} %copy-done.38), channel_id=1, source_target_pairs={{0,6},{1,7},{2,0},{3,1},{4,2},{5,3},{6,4},{7,5},{8,14},{9,15},{10,... | collective-permute-start | bytes 589832 | tf_op jit(solution)/shard_map/reduce/ppermute | solution.py:39
  205.5 2.9 %collective-permute-start.45 = (bf16[1536,128]{1,0:T(8,128)(2,1)S(1)}, bf16[1536,128]{1,0:T(8,128)(2,1)S(1)}, u32[]{:S(2)}, u32[]{:S(2)}) collective-permute-start(bf16[1536,128]{1,0:T(8,128)(2,1)S(1)} %pad_maximum_fusion.5), channel_id=1, source_target_pairs={{0,6},{1,7},{2,0},{3,1},{4,2},{5,3},{6,4},{7,5},{8,14},{9,15},{10,... | collective-permute-start | bytes 1179656 | tf_op jit(solution)/shard_map/reduce/ppermute | solution.py:39
  208.8 2.7 %collective-permute-start.35 = (bf16[1536,128]{1,0:T(8,128)(2,1)S(1)}, bf16[1536,128]{1,0:T(8,128)(2,1)S(1)}, u32[]{:S(2)}, u32[]{:S(2)}) collective-permute-start(bf16[1536,128]{1,0:T(8,128)(2,1)S(1)} %pad_maximum_fusion.3), channel_id=1, source_target_pairs={{0,6},{1,7},{2,0},{3,1},{4,2},{5,3},{6,4},{7,5},{8,14},{9,15},{10,... | collective-permute-start | bytes 1179656 | tf_op jit(solution)/shard_map/reduce/ppermute | solution.py:39
  211.8 4.0 %collective-permute-done.43 = bf16[1536,128]{1,0:T(8,128)(2,1)S(1)} collective-permute-done((bf16[1536,128]{1,0:T(8,128)(2,1)S(1)}, bf16[1536,128]{1,0:T(8,128)(2,1)S(1)}, u32[]{:S(2)}, u32[]{:S(2)}) %collective-permute-start.43) | collective-permute-done | bytes 393248 | tf_op jit(solution)/shard_map/reduce/ppermute | solution.py:39
  216.7 8.8 %collective-permute-start.48 = (bf16[768,128]{1,0:T(8,128)(2,1)S(1)}, bf16[768,128]{1,0:T(8,128)(2,1)S(1)}, u32[]{:S(2)}, u32[]{:S(2)}) collective-permute-start(bf16[768,128]{1,0:T(8,128)(2,1)S(1)} %get-tuple-element.44), channel_id=1, source_target_pairs={{0,8},{1,9},{2,10},{3,11},{4,12},{5,13},{6,14},{7,15},{8,0},{9,1},... | collective-permute-start | bytes 589832 | tf_op jit(solution)/shard_map/reduce/ppermute | solution.py:39
  226.4 7.2 %collective-permute-start.47 = (bf16[768,128]{1,0:T(8,128)(2,1)S(1)}, bf16[768,128]{1,0:T(8,128)(2,1)S(1)}, u32[]{:S(2)}, u32[]{:S(2)}) collective-permute-start(bf16[768,128]{1,0:T(8,128)(2,1)S(1)} %get-tuple-element.46), channel_id=1, source_target_pairs={{0,8},{1,9},{2,10},{3,11},{4,12},{5,13},{6,14},{7,15},{8,0},{9,1},... | collective-permute-start | bytes 589832 | tf_op jit(solution)/shard_map/reduce/ppermute | solution.py:39
  234.5 3.5 %collective-permute-start.46 = (bf16[768,128]{1,0:T(8,128)(2,1)S(1)}, bf16[768,128]{1,0:T(8,128)(2,1)S(1)}, u32[]{:S(2)}, u32[]{:S(2)}) collective-permute-start(bf16[768,128]{1,0:T(8,128)(2,1)S(1)} %get-tuple-element.48), channel_id=1, source_target_pairs={{0,8},{1,9},{2,10},{3,11},{4,12},{5,13},{6,14},{7,15},{8,0},{9,1},... | collective-permute-start | bytes 589832 | tf_op jit(solution)/shard_map/reduce/ppermute | solution.py:39
  238.0 1.0 collective-permute-done.46.g0
  239.7 3.7 %finish.1 = bf16[768,768]{1,0:T(8,128)(2,1)} custom-call(bf16[768,128]{1,0:T(8,128)(2,1)} %get-tuple-element.49.k0, bf16[768,128]{1,0:T(8,128)(2,1)} %get-tuple-element.47.k1, bf16[768,128]{1,0:T(8,128)(2,1)} %get-tuple-element.45.k2, bf16[768,128]{1,0:T(8,128)(2,1)} %copy-done.41, bf16[768,128]{1,0:T(8,128)(2,1)} %copy-done.40, bf16[768,128]{1,0:T(8,128)(2,1)} %copy-done.39), custom_call_target="tpu_custom_call" | custom-call | flops 905969664 | bytes 4194304 | tf_op jit(solution)/shard_map/finish/pallas_call | solution.py:302
  (177 shorter events, 14.7 us)
Async XLA Ops:
  0.0 12.9 %copy-start.29 = (s32[512]{0:T(512)S(1)}, s32[512]{0:T(512)}, u32[]{:S(2)}) copy-start(s32[512]{0:T(512)} %param.10) | copy-start | bytes 6148
  0.0 13.0 %collective-permute-start.3 = (s32[8]{0:T(128)}, s32[8]{0:T(128)S(1)}, u32[]{:S(2)}, u32[]{:S(2)}) collective-permute-start(s32[8]{0:T(128)} %req_own.1), channel_id=1, source_target_pairs={{0,120},{1,121},{2,122},{3,123},{4,124},{5,125},{6,126},{7,127},{8... | collective-permute-start | bytes 104 | tf_op jit(solution)/shard_map/density/ppermute | solution.py:60
  1.4 13.6 %collective-permute-start.4 = (s32[8]{0:T(128)}, s32[8]{0:T(128)S(1)}, u32[]{:S(2)}, u32[]{:S(2)}) collective-permute-start(s32[8]{0:T(128)} %req_own.1), channel_id=1, source_target_pairs={{0,8},{1,9},{2,10},{3,11},{4,12},{5,13},{6,14},{7,15},{8,16},{9,17... | collective-permute-start | bytes 104 | tf_op jit(solution)/shard_map/density/ppermute | solution.py:60
  2.8 5.0 %collective-permute-start.5 = (bf16[40,1024]{1,0:T(8,128)(2,1)}, bf16[40,1024]{1,0:T(8,128)(2,1)S(1)}, u32[]{:S(2)}, u32[]{:S(2)}) collective-permute-start(bf16[40,1024]{1,0:T(8,128)(2,1)} %param.11), channel_id=1, source_target_pairs={{0,1},{1,0},{2,3},{3,2},{4,5},{5,4},{6,7},{7,6},{8,9},{9,8},{10,11... | collective-permute-start | bytes 245768 | tf_op jit(solution)/shard_map/density/ppermute | solution.py:39
  7.8 11.3 %copy-start.11 = (bf16[80,1024]{1,0:T(8,128)(2,1)}, bf16[80,1024]{1,0:T(8,128)(2,1)S(1)}, u32[]{:S(2)}) copy-start(bf16[80,1024]{1,0:T(8,128)(2,1)S(1)} %constant_dynamic-update-slice_fusion.p0) | copy-start | bytes 491524
  7.8 8.0 %collective-permute-start.6 = (bf16[80,1024]{1,0:T(8,128)(2,1)S(1)}, bf16[80,1024]{1,0:T(8,128)(2,1)S(1)}, u32[]{:S(2)}, u32[]{:S(2)}) collective-permute-start(bf16[80,1024]{1,0:T(8,128)(2,1)S(1)} %constant_dynamic-update-slice_fusion.p0), channel_id=1, source_target_pairs={{0,2},{1,3},{2,4},{3,5},{4,6},{5,7},{6,0},{7,1},{8,10},{9,11},{10,... | collective-permute-start | bytes 491528 | tf_op jit(solution)/shard_map/density/ppermute | solution.py:39
  9.5 9.6 %collective-permute-start.7 = (bf16[80,1024]{1,0:T(8,128)(2,1)S(1)}, bf16[80,1024]{1,0:T(8,128)(2,1)S(1)}, u32[]{:S(2)}, u32[]{:S(2)}) collective-permute-start(bf16[80,1024]{1,0:T(8,128)(2,1)S(1)} %constant_dynamic-update-slice_fusion.p0), channel_id=1, source_target_pairs={{0,6},{1,7},{2,0},{3,1},{4,2},{5,3},{6,4},{7,5},{8,14},{9,15},{10,... | collective-permute-start | bytes 491528 | tf_op jit(solution)/shard_map/density/ppermute | solution.py:39
  11.7 7.4 %collective-permute-start.8 = (bf16[80,1024]{1,0:T(8,128)(2,1)S(1)}, bf16[80,1024]{1,0:T(8,128)(2,1)S(1)}, u32[]{:S(2)}, u32[]{:S(2)}) collective-permute-start(bf16[80,1024]{1,0:T(8,128)(2,1)S(1)} %constant_dynamic-update-slice_fusion.p0), channel_id=1, source_target_pairs={{0,4},{1,5},{2,6},{3,7},{4,0},{5,1},{6,2},{7,3},{8,12},{9,13},{10,... | collective-permute-start | bytes 491528 | tf_op jit(solution)/shard_map/density/ppermute | solution.py:39
  13.0 41.6 %collective-permute-start.36 = (bf16[1536,128]{1,0:T(8,128)(2,1)S(1)}, bf16[1536,128]{1,0:T(8,128)(2,1)S(1)}, u32[]{:S(2)}, u32[]{:S(2)}) collective-permute-start(bf16[1536,128]{1,0:T(8,128)(2,1)S(1)} %get-tuple-element.41), channel_id=1, source_target_pairs={{0,16},{1,0},{2,18},{3,2},{4,20},{5,4},{6,22},{7,6},{8,24},{9,8},{... | collective-permute-start | bytes 1179656 | tf_op jit(solution)/shard_map/gather/ppermute | solution.py:39
  15.1 41.7 %collective-permute-start.37 = (bf16[1536,128]{1,0:T(8,128)(2,1)S(1)}, bf16[1536,128]{1,0:T(8,128)(2,1)S(1)}, u32[]{:S(2)}, u32[]{:S(2)}) collective-permute-start(bf16[1536,128]{1,0:T(8,128)(2,1)S(1)} %get-tuple-element.41), channel_id=1, source_target_pairs={{0,0},{1,16},{2,2},{3,18},{4,4},{5,20},{6,6},{7,22},{8,8},{9,24},{... | collective-permute-start | bytes 1179656 | tf_op jit(solution)/shard_map/gather/ppermute | solution.py:39
  15.8 39.2 %collective-permute-start.26 = (bf16[1536,128]{1,0:T(8,128)(2,1)S(1)}, bf16[1536,128]{1,0:T(8,128)(2,1)}, u32[]{:S(2)}, u32[]{:S(2)}) collective-permute-start(bf16[1536,128]{1,0:T(8,128)(2,1)S(1)} %get-tuple-element.43), channel_id=1, source_target_pairs={{0,16},{1,0},{2,18},{3,2},{4,20},{5,4},{6,22},{7,6},{8,24},{9,8},{... | collective-permute-start | bytes 1179656 | tf_op jit(solution)/shard_map/gather/ppermute | solution.py:39
  22.6 13.0 %collective-permute-start.10 = (bf16[16,1024]{1,0:T(8,128)(2,1)}, bf16[16,1024]{1,0:T(8,128)(2,1)S(1)}, u32[]{:S(2)}, u32[]{:S(2)}) collective-permute-start(bf16[16,1024]{1,0:T(8,128)(2,1)} %get-tuple-element.25), channel_id=1, source_target_pairs={{0,120},{1,121},{2,122},{3,123},{4,124},{5,125},{6,126},{7,127},{8... | collective-permute-start | bytes 98312 | tf_op jit(solution)/shard_map/density/ppermute | solution.py:60
  26.0 10.3 %collective-permute-start.9 = (bf16[16,1024]{1,0:T(8,128)(2,1)}, bf16[16,1024]{1,0:T(8,128)(2,1)S(1)}, u32[]{:S(2)}, u32[]{:S(2)}) collective-permute-start(bf16[16,1024]{1,0:T(8,128)(2,1)} %get-tuple-element.24), channel_id=1, source_target_pairs={{0,8},{1,9},{2,10},{3,11},{4,12},{5,13},{6,14},{7,15},{8,16},{9,17... | collective-permute-start | bytes 98312 | tf_op jit(solution)/shard_map/density/ppermute | solution.py:60
  35.6 23.9 %collective-permute-start.27 = (bf16[1536,128]{1,0:T(8,128)(2,1)S(1)}, bf16[1536,128]{1,0:T(8,128)(2,1)S(1)}, u32[]{:S(2)}, u32[]{:S(2)}) collective-permute-start(bf16[1536,128]{1,0:T(8,128)(2,1)S(1)} %get-tuple-element.43), channel_id=1, source_target_pairs={{0,0},{1,16},{2,2},{3,18},{4,4},{5,20},{6,6},{7,22},{8,8},{9,24},{... | collective-permute-start | bytes 1179656 | tf_op jit(solution)/shard_map/gather/ppermute | solution.py:39
  36.9 13.4 %copy-start.1 = (bf16[512,1024]{1,0:T(8,128)(2,1)S(1)}, bf16[512,1024]{1,0:T(8,128)(2,1)}, u32[]{:S(2)}) copy-start(bf16[512,1024]{1,0:T(8,128)(2,1)} %param.9) | copy-start | bytes 3145732
  48.5 4.3 %collective-permute-start.11 = (bf16[8,1152]{1,0:T(8,128)(2,1)}, bf16[8,1152]{1,0:T(8,128)(2,1)S(1)}, u32[]{:S(2)}, u32[]{:S(2)}) collective-permute-start(bf16[8,1152]{1,0:T(8,128)(2,1)} %terms.1), channel_id=1, source_target_pairs={{0,1},{1,0},{2,3},{3,2},{4,5},{5,4},{6,7},{7,6},{8,9},{9,8},{10,11... | collective-permute-start | bytes 55304 | tf_op jit(solution)/shard_map/terms/ppermute | solution.py:39
  50.4 41.6 %copy-start = (bf16[512,1152]{1,0:T(8,128)(2,1)}, bf16[512,1152]{1,0:T(8,128)(2,1)S(1)}, u32[]{:S(2)}) copy-start(bf16[512,1152]{1,0:T(8,128)(2,1)S(1)} %fusion.1.f0) | copy-start | bytes 3538948
  52.8 41.4 %collective-permute-start = (bf16[512,1152]{1,0:T(8,128)(2,1)S(1)}, bf16[512,1152]{1,0:T(8,128)(2,1)}, u32[]{:S(2)}, u32[]{:S(2)}) collective-permute-start(bf16[512,1152]{1,0:T(8,128)(2,1)S(1)} %fusion.1.f0), channel_id=1, source_target_pairs={{0,1},{1,0},{2,3},{3,2},{4,5},{5,4},{6,7},{7,6},{8,9},{9,8},{10,11... | collective-permute-start | bytes 3538952 | tf_op jit(solution)/shard_map/fock/ppermute | solution.py:39
  54.6 34.3 %collective-permute-start.16 = (bf16[1536,128]{1,0:T(8,128)(2,1)S(1)}, bf16[1536,128]{1,0:T(8,128)(2,1)S(1)}, u32[]{:S(2)}, u32[]{:S(2)}) collective-permute-start(bf16[1536,128]{1,0:T(8,128)(2,1)S(1)} %get-tuple-element.42), channel_id=1, source_target_pairs={{0,16},{1,0},{2,18},{3,2},{4,20},{5,4},{6,22},{7,6},{8,24},{9,8},{... | collective-permute-start | bytes 1179656 | tf_op jit(solution)/shard_map/gather/ppermute | solution.py:39
  54.9 4.5 %collective-permute-start.12 = (bf16[16,1152]{1,0:T(8,128)(2,1)S(1)}, bf16[16,1152]{1,0:T(8,128)(2,1)S(1)}, u32[]{:S(2)}, u32[]{:S(2)}) collective-permute-start(bf16[16,1152]{1,0:T(8,128)(2,1)S(1)} %pad_maximum_fusion.6.t0), channel_id=1, source_target_pairs={{0,2},{1,3},{2,4},{3,5},{4,6},{5,7},{6,0},{7,1},{8,10},{9,11},{10,... | collective-permute-start | bytes 110600 | tf_op jit(solution)/shard_map/terms/ppermute | solution.py:39
  56.8 4.6 %collective-permute-start.13 = (bf16[16,1152]{1,0:T(8,128)(2,1)S(1)}, bf16[16,1152]{1,0:T(8,128)(2,1)S(1)}, u32[]{:S(2)}, u32[]{:S(2)}) collective-permute-start(bf16[16,1152]{1,0:T(8,128)(2,1)S(1)} %pad_maximum_fusion.6.t0), channel_id=1, source_target_pairs={{0,6},{1,7},{2,0},{3,1},{4,2},{5,3},{6,4},{7,5},{8,14},{9,15},{10,... | collective-permute-start | bytes 110600 | tf_op jit(solution)/shard_map/terms/ppermute | solution.py:39
  58.8 38.6 %copy-start.17 = (bf16[3072,128]{1,0:T(8,128)(2,1)}, bf16[3072,128]{1,0:T(8,128)(2,1)S(1)}, u32[]{:S(2)}) copy-start(bf16[3072,128]{1,0:T(8,128)(2,1)S(1)} %constant_dynamic-update-slice_fusion.11.own) | copy-start | bytes 2359300
  59.4 49.8 %copy-start.24 = (bf16[16,1152]{1,0:T(8,128)(2,1)}, bf16[16,1152]{1,0:T(8,128)(2,1)S(1)}, u32[]{:S(2)}) copy-start(bf16[16,1152]{1,0:T(8,128)(2,1)S(1)} %collective-permute-done.12.t1) | copy-start | bytes 110596
  59.4 4.7 %collective-permute-start.14 = (bf16[16,1152]{1,0:T(8,128)(2,1)S(1)}, bf16[16,1152]{1,0:T(8,128)(2,1)S(1)}, u32[]{:S(2)}, u32[]{:S(2)}) collective-permute-start(bf16[16,1152]{1,0:T(8,128)(2,1)S(1)} %pad_maximum_fusion.6.t0), channel_id=1, source_target_pairs={{0,4},{1,5},{2,6},{3,7},{4,0},{5,1},{6,2},{7,3},{8,12},{9,13},{10,... | collective-permute-start | bytes 110600 | tf_op jit(solution)/shard_map/terms/ppermute | solution.py:39
  59.5 35.5 %collective-permute-start.38 = (bf16[3072,128]{1,0:T(8,128)(2,1)S(1)}, bf16[3072,128]{1,0:T(8,128)(2,1)S(1)}, u32[]{:S(2)}, u32[]{:S(2)}) collective-permute-start(bf16[3072,128]{1,0:T(8,128)(2,1)S(1)} %constant_dynamic-update-slice_fusion.11.own), channel_id=1, source_target_pairs={{0,32},{1,33},{2,34},{3,35},{4,36},{5,37},{6,38},{7,39},{8,40},{9,... | collective-permute-start | bytes 2359304 | tf_op jit(solution)/shard_map/gather/ppermute | solution.py:39
  61.4 47.9 %copy-start.16 = (bf16[3072,128]{1,0:T(8,128)(2,1)}, bf16[3072,128]{1,0:T(8,128)(2,1)S(1)}, u32[]{:S(2)}) copy-start(bf16[3072,128]{1,0:T(8,128)(2,1)S(1)} %constant_dynamic-update-slice_fusion.9.own) | copy-start | bytes 2359300
  61.4 52.4 %copy-start.25 = (bf16[16,1152]{1,0:T(8,128)(2,1)}, bf16[16,1152]{1,0:T(8,128)(2,1)S(1)}, u32[]{:S(2)}) copy-start(bf16[16,1152]{1,0:T(8,128)(2,1)S(1)} %collective-permute-done.13.t2) | copy-start | bytes 110596
  61.4 30.6 %collective-permute-start.17 = (bf16[1536,128]{1,0:T(8,128)(2,1)S(1)}, bf16[1536,128]{1,0:T(8,128)(2,1)S(1)}, u32[]{:S(2)}, u32[]{:S(2)}) collective-permute-start(bf16[1536,128]{1,0:T(8,128)(2,1)S(1)} %get-tuple-element.42), channel_id=1, source_target_pairs={{0,0},{1,16},{2,2},{3,18},{4,4},{5,20},{6,6},{7,22},{8,8},{9,24},{... | collective-permute-start | bytes 1179656 | tf_op jit(solution)/shard_map/gather/ppermute | solution.py:39
  64.1 53.1 %copy-start.26 = (bf16[16,1152]{1,0:T(8,128)(2,1)}, bf16[16,1152]{1,0:T(8,128)(2,1)S(1)}, u32[]{:S(2)}) copy-start(bf16[16,1152]{1,0:T(8,128)(2,1)S(1)} %collective-permute-done.14.t3) | copy-start | bytes 110596
  64.1 33.3 %collective-permute-start.39 = (bf16[3072,128]{1,0:T(8,128)(2,1)S(1)}, bf16[3072,128]{1,0:T(8,128)(2,1)S(1)}, u32[]{:S(2)}, u32[]{:S(2)}) collective-permute-start(bf16[3072,128]{1,0:T(8,128)(2,1)S(1)} %constant_dynamic-update-slice_fusion.11.own), channel_id=1, source_target_pairs={{0,96},{1,97},{2,98},{3,99},{4,100},{5,101},{6,102},{7,103},{8,104... | collective-permute-start | bytes 2359304 | tf_op jit(solution)/shard_map/gather/ppermute | solution.py:39
  88.9 19.1 %collective-permute-start.28 = (bf16[3072,128]{1,0:T(8,128)(2,1)S(1)}, bf16[3072,128]{1,0:T(8,128)(2,1)S(1)}, u32[]{:S(2)}, u32[]{:S(2)}) collective-permute-start(bf16[3072,128]{1,0:T(8,128)(2,1)S(1)} %constant_dynamic-update-slice_fusion.9.own), channel_id=1, source_target_pairs={{0,32},{1,33},{2,34},{3,35},{4,36},{5,37},{6,38},{7,39},{8,40},{9,... | collective-permute-start | bytes 2359304 | tf_op jit(solution)/shard_map/gather/ppermute | solution.py:39
  92.0 41.3 %collective-permute-start.1 = (bf16[512,1152]{1,0:T(8,128)(2,1)S(1)}, bf16[512,1152]{1,0:T(8,128)(2,1)}, u32[]{:S(2)}, u32[]{:S(2)}) collective-permute-start(bf16[512,1152]{1,0:T(8,128)(2,1)S(1)} %fusion.1.f0), channel_id=1, source_target_pairs={{0,8},{1,9},{2,10},{3,11},{4,12},{5,13},{6,14},{7,15},{8,0},{9,1},... | collective-permute-start | bytes 3538952 | tf_op jit(solution)/shard_map/fock/ppermute | solution.py:39
  94.2 41.7 %collective-permute-start.2 = (bf16[512,1152]{1,0:T(8,128)(2,1)}, bf16[512,1152]{1,0:T(8,128)(2,1)}, u32[]{:S(2)}, u32[]{:S(2)}) collective-permute-start(bf16[512,1152]{1,0:T(8,128)(2,1)} %collective-permute-done.f1), channel_id=1, source_target_pairs={{0,8},{1,9},{2,10},{3,11},{4,12},{5,13},{6,14},{7,15},{8,0},{9,1},... | collective-permute-start | bytes 3538952 | tf_op jit(solution)/shard_map/fock/ppermute | solution.py:39
  95.0 22.9 %copy-start.13 = (bf16[3072,128]{1,0:T(8,128)(2,1)}, bf16[3072,128]{1,0:T(8,128)(2,1)S(1)}, u32[]{:S(2)}) copy-start(bf16[3072,128]{1,0:T(8,128)(2,1)S(1)} %collective-permute-done.38.left) | copy-start | bytes 2359300
  95.0 18.8 %collective-permute-start.29 = (bf16[3072,128]{1,0:T(8,128)(2,1)S(1)}, bf16[3072,128]{1,0:T(8,128)(2,1)}, u32[]{:S(2)}, u32[]{:S(2)}) collective-permute-start(bf16[3072,128]{1,0:T(8,128)(2,1)S(1)} %constant_dynamic-update-slice_fusion.9.own), channel_id=1, source_target_pairs={{0,96},{1,97},{2,98},{3,99},{4,100},{5,101},{6,102},{7,103},{8,104... | collective-permute-start | bytes 2359304 | tf_op jit(solution)/shard_map/gather/ppermute | solution.py:39
  97.5 10.5 %copy-start.14 = (bf16[3072,128]{1,0:T(8,128)(2,1)}, bf16[3072,128]{1,0:T(8,128)(2,1)S(1)}, u32[]{:S(2)}) copy-start(bf16[3072,128]{1,0:T(8,128)(2,1)S(1)} %collective-permute-done.39.right) | copy-start | bytes 2359300
  97.5 27.5 %collective-permute-start.18 = (bf16[3072,128]{1,0:T(8,128)(2,1)}, bf16[3072,128]{1,0:T(8,128)(2,1)}, u32[]{:S(2)}, u32[]{:S(2)}) collective-permute-start(bf16[3072,128]{1,0:T(8,128)(2,1)} %constant_dynamic-update-slice_fusion.7.own), channel_id=1, source_target_pairs={{0,32},{1,33},{2,34},{3,35},{4,36},{5,37},{6,38},{7,39},{8,40},{9,... | collective-permute-start | bytes 2359304 | tf_op jit(solution)/shard_map/gather/ppermute | solution.py:39
  108.0 10.0 %copy-start.12 = (bf16[3072,128]{1,0:T(8,128)(2,1)}, bf16[3072,128]{1,0:T(8,128)(2,1)S(1)}, u32[]{:S(2)}) copy-start(bf16[3072,128]{1,0:T(8,128)(2,1)S(1)} %collective-permute-done.28.left) | copy-start | bytes 2359300
  108.0 21.4 %collective-permute-start.19 = (bf16[3072,128]{1,0:T(8,128)(2,1)}, bf16[3072,128]{1,0:T(8,128)(2,1)}, u32[]{:S(2)}, u32[]{:S(2)}) collective-permute-start(bf16[3072,128]{1,0:T(8,128)(2,1)} %constant_dynamic-update-slice_fusion.7.own), channel_id=1, source_target_pairs={{0,96},{1,97},{2,98},{3,99},{4,100},{5,101},{6,102},{7,103},{8,104... | collective-permute-start | bytes 2359304 | tf_op jit(solution)/shard_map/gather/ppermute | solution.py:39
  109.3 8.6 %copy-start.15 = (bf16[3072,128]{1,0:T(8,128)(2,1)S(1)}, bf16[3072,128]{1,0:T(8,128)(2,1)}, u32[]{:S(2)}) copy-start(bf16[3072,128]{1,0:T(8,128)(2,1)} %copy-done.14) | copy-start | bytes 2359300
  113.8 19.3 %collective-permute-start.15 = (bf16[64,1152]{1,0:T(8,128)(2,1)}, bf16[64,1152]{1,0:T(8,128)(2,1)}, u32[]{:S(2)}, u32[]{:S(2)}) collective-permute-start(bf16[64,1152]{1,0:T(8,128)(2,1)} %constant_dynamic-update-slice_fusion.2), channel_id=1, source_target_pairs={{0,8},{1,9},{2,10},{3,11},{4,12},{5,13},{6,14},{7,15},{8,0},{9,1},... | collective-permute-start | bytes 442376 | tf_op jit(solution)/shard_map/terms/ppermute | solution.py:39
  124.9 28.6 %collective-permute-start.40 = (bf16[1536,128]{1,0:T(8,128)(2,1)S(1)}, bf16[1536,128]{1,0:T(8,128)(2,1)S(1)}, u32[]{:S(2)}, u32[]{:S(2)}) collective-permute-start(bf16[1536,128]{1,0:T(8,128)(2,1)S(1)} %slice.88), channel_id=1, source_target_pairs={{0,32},{1,33},{2,34},{3,35},{4,36},{5,37},{6,38},{7,39},{8,40},{9,... | collective-permute-start | bytes 1179656 | tf_op jit(solution)/shard_map/gather/ppermute | solution.py:39
  129.4 26.9 %collective-permute-start.41 = (bf16[1536,128]{1,0:T(8,128)(2,1)S(1)}, bf16[1536,128]{1,0:T(8,128)(2,1)S(1)}, u32[]{:S(2)}, u32[]{:S(2)}) collective-permute-start(bf16[1536,128]{1,0:T(8,128)(2,1)S(1)} %slice.89), channel_id=1, source_target_pairs={{0,96},{1,97},{2,98},{3,99},{4,100},{5,101},{6,102},{7,103},{8,104... | collective-permute-start | bytes 1179656 | tf_op jit(solution)/shard_map/gather/ppermute | solution.py:39
  133.2 37.7 %collective-permute-start.30 = (bf16[1536,128]{1,0:T(8,128)(2,1)S(1)}, bf16[1536,128]{1,0:T(8,128)(2,1)S(1)}, u32[]{:S(2)}, u32[]{:S(2)}) collective-permute-start(bf16[1536,128]{1,0:T(8,128)(2,1)S(1)} %slice.86), channel_id=1, source_target_pairs={{0,32},{1,33},{2,34},{3,35},{4,36},{5,37},{6,38},{7,39},{8,40},{9,... | collective-permute-start | bytes 1179656 | tf_op jit(solution)/shard_map/gather/ppermute | solution.py:39
  133.3 39.6 %collective-permute-start.31 = (bf16[1536,128]{1,0:T(8,128)(2,1)S(1)}, bf16[1536,128]{1,0:T(8,128)(2,1)S(1)}, u32[]{:S(2)}, u32[]{:S(2)}) collective-permute-start(bf16[1536,128]{1,0:T(8,128)(2,1)S(1)} %slice.87), channel_id=1, source_target_pairs={{0,96},{1,97},{2,98},{3,99},{4,100},{5,101},{6,102},{7,103},{8,104... | collective-permute-start | bytes 1179656 | tf_op jit(solution)/shard_map/gather/ppermute | solution.py:39
  135.9 49.9 %collective-permute-start.20 = (bf16[1536,128]{1,0:T(8,128)(2,1)S(1)}, bf16[1536,128]{1,0:T(8,128)(2,1)S(1)}, u32[]{:S(2)}, u32[]{:S(2)}) collective-permute-start(bf16[1536,128]{1,0:T(8,128)(2,1)S(1)} %slice.84), channel_id=1, source_target_pairs={{0,32},{1,33},{2,34},{3,35},{4,36},{5,37},{6,38},{7,39},{8,40},{9,... | collective-permute-start | bytes 1179656 | tf_op jit(solution)/shard_map/gather/ppermute | solution.py:39
  153.6 35.0 %collective-permute-start.21 = (bf16[1536,128]{1,0:T(8,128)(2,1)S(1)}, bf16[1536,128]{1,0:T(8,128)(2,1)S(1)}, u32[]{:S(2)}, u32[]{:S(2)}) collective-permute-start(bf16[1536,128]{1,0:T(8,128)(2,1)S(1)} %slice.85), channel_id=1, source_target_pairs={{0,96},{1,97},{2,98},{3,99},{4,100},{5,101},{6,102},{7,103},{8,104... | collective-permute-start | bytes 1179656 | tf_op jit(solution)/shard_map/gather/ppermute | solution.py:39
  168.1 34.4 %collective-permute-start.42 = (bf16[768,128]{1,0:T(8,128)(2,1)}, bf16[768,128]{1,0:T(8,128)(2,1)S(1)}, u32[]{:S(2)}, u32[]{:S(2)}) collective-permute-start(bf16[768,128]{1,0:T(8,128)(2,1)} %get-tuple-element.38), channel_id=1, source_target_pairs={{0,2},{1,3},{2,4},{3,5},{4,6},{5,7},{6,0},{7,1},{8,10},{9,11},{10,... | collective-permute-start | bytes 589832 | tf_op jit(solution)/shard_map/reduce/ppermute | solution.py:39
  170.8 34.5 %collective-permute-start.44 = (bf16[768,128]{1,0:T(8,128)(2,1)}, bf16[768,128]{1,0:T(8,128)(2,1)S(1)}, u32[]{:S(2)}, u32[]{:S(2)}) collective-permute-start(bf16[768,128]{1,0:T(8,128)(2,1)} %get-tuple-element.40), channel_id=1, source_target_pairs={{0,6},{1,7},{2,0},{3,1},{4,2},{5,3},{6,4},{7,5},{8,14},{9,15},{10,... | collective-permute-start | bytes 589832 | tf_op jit(solution)/shard_map/reduce/ppermute | solution.py:39
  184.8 20.7 %collective-permute-start.32 = (bf16[768,128]{1,0:T(8,128)(2,1)}, bf16[768,128]{1,0:T(8,128)(2,1)S(1)}, u32[]{:S(2)}, u32[]{:S(2)}) collective-permute-start(bf16[768,128]{1,0:T(8,128)(2,1)} %get-tuple-element.33), channel_id=1, source_target_pairs={{0,2},{1,3},{2,4},{3,5},{4,6},{5,7},{6,0},{7,1},{8,10},{9,11},{10,... | collective-permute-start | bytes 589832 | tf_op jit(solution)/shard_map/reduce/ppermute | solution.py:39
  185.8 14.6 %copy-start.3 = (bf16[1536,128]{1,0:T(8,128)(2,1)S(1)}, bf16[1536,128]{1,0:T(8,128)(2,1)}, u32[]{:S(2)}) copy-start(bf16[1536,128]{1,0:T(8,128)(2,1)} %get-tuple-element.34) | copy-start | bytes 1179652
  185.8 22.7 %collective-permute-start.34 = (bf16[768,128]{1,0:T(8,128)(2,1)}, bf16[768,128]{1,0:T(8,128)(2,1)S(1)}, u32[]{:S(2)}, u32[]{:S(2)}) collective-permute-start(bf16[768,128]{1,0:T(8,128)(2,1)} %get-tuple-element.35), channel_id=1, source_target_pairs={{0,6},{1,7},{2,0},{3,1},{4,2},{5,3},{6,4},{7,5},{8,14},{9,15},{10,... | collective-permute-start | bytes 589832 | tf_op jit(solution)/shard_map/reduce/ppermute | solution.py:39
  200.5 8.3 %collective-permute-start.22 = (bf16[768,128]{1,0:T(8,128)(2,1)}, bf16[768,128]{1,0:T(8,128)(2,1)S(1)}, u32[]{:S(2)}, u32[]{:S(2)}) collective-permute-start(bf16[768,128]{1,0:T(8,128)(2,1)} %get-tuple-element.28), channel_id=1, source_target_pairs={{0,2},{1,3},{2,4},{3,5},{4,6},{5,7},{6,0},{7,1},{8,10},{9,11},{10,... | collective-permute-start | bytes 589832 | tf_op jit(solution)/shard_map/reduce/ppermute | solution.py:39
  202.6 9.0 %collective-permute-start.24 = (bf16[768,128]{1,0:T(8,128)(2,1)S(1)}, bf16[768,128]{1,0:T(8,128)(2,1)S(1)}, u32[]{:S(2)}, u32[]{:S(2)}) collective-permute-start(bf16[768,128]{1,0:T(8,128)(2,1)S(1)} %copy-done.38), channel_id=1, source_target_pairs={{0,6},{1,7},{2,0},{3,1},{4,2},{5,3},{6,4},{7,5},{8,14},{9,15},{10,... | collective-permute-start | bytes 589832 | tf_op jit(solution)/shard_map/reduce/ppermute | solution.py:39
  205.3 10.5 %collective-permute-start.43 = (bf16[1536,128]{1,0:T(8,128)(2,1)S(1)}, bf16[1536,128]{1,0:T(8,128)(2,1)S(1)}, u32[]{:S(2)}, u32[]{:S(2)}) collective-permute-start(bf16[1536,128]{1,0:T(8,128)(2,1)S(1)} %pad_maximum_fusion.4), channel_id=1, source_target_pairs={{0,2},{1,3},{2,4},{3,5},{4,6},{5,7},{6,0},{7,1},{8,10},{9,11},{10,... | collective-permute-start | bytes 1179656 | tf_op jit(solution)/shard_map/reduce/ppermute | solution.py:39
  205.5 10.3 %collective-permute-start.45 = (bf16[1536,128]{1,0:T(8,128)(2,1)S(1)}, bf16[1536,128]{1,0:T(8,128)(2,1)S(1)}, u32[]{:S(2)}, u32[]{:S(2)}) collective-permute-start(bf16[1536,128]{1,0:T(8,128)(2,1)S(1)} %pad_maximum_fusion.5), channel_id=1, source_target_pairs={{0,6},{1,7},{2,0},{3,1},{4,2},{5,3},{6,4},{7,5},{8,14},{9,15},{10,... | collective-permute-start | bytes 1179656 | tf_op jit(solution)/shard_map/reduce/ppermute | solution.py:39
  208.6 16.9 %collective-permute-start.33 = (bf16[1536,128]{1,0:T(8,128)(2,1)S(1)}, bf16[1536,128]{1,0:T(8,128)(2,1)S(1)}, u32[]{:S(2)}, u32[]{:S(2)}) collective-permute-start(bf16[1536,128]{1,0:T(8,128)(2,1)S(1)} %pad_maximum_fusion.2), channel_id=1, source_target_pairs={{0,2},{1,3},{2,4},{3,5},{4,6},{5,7},{6,0},{7,1},{8,10},{9,11},{10,... | collective-permute-start | bytes 1179656 | tf_op jit(solution)/shard_map/reduce/ppermute | solution.py:39
  208.8 16.7 %collective-permute-start.35 = (bf16[1536,128]{1,0:T(8,128)(2,1)S(1)}, bf16[1536,128]{1,0:T(8,128)(2,1)S(1)}, u32[]{:S(2)}, u32[]{:S(2)}) collective-permute-start(bf16[1536,128]{1,0:T(8,128)(2,1)S(1)} %pad_maximum_fusion.3), channel_id=1, source_target_pairs={{0,6},{1,7},{2,0},{3,1},{4,2},{5,3},{6,4},{7,5},{8,14},{9,15},{10,... | collective-permute-start | bytes 1179656 | tf_op jit(solution)/shard_map/reduce/ppermute | solution.py:39
  211.6 22.0 %collective-permute-start.23 = (bf16[1536,128]{1,0:T(8,128)(2,1)S(1)}, bf16[1536,128]{1,0:T(8,128)(2,1)S(1)}, u32[]{:S(2)}, u32[]{:S(2)}) collective-permute-start(bf16[1536,128]{1,0:T(8,128)(2,1)S(1)} %pad_maximum_fusion), channel_id=1, source_target_pairs={{0,2},{1,3},{2,4},{3,5},{4,6},{5,7},{6,0},{7,1},{8,10},{9,11},{10,... | collective-permute-start | bytes 1179656 | tf_op jit(solution)/shard_map/reduce/ppermute | solution.py:39
  215.8 17.8 %collective-permute-start.25 = (bf16[1536,128]{1,0:T(8,128)(2,1)S(1)}, bf16[1536,128]{1,0:T(8,128)(2,1)S(1)}, u32[]{:S(2)}, u32[]{:S(2)}) collective-permute-start(bf16[1536,128]{1,0:T(8,128)(2,1)S(1)} %pad_maximum_fusion.1), channel_id=1, source_target_pairs={{0,6},{1,7},{2,0},{3,1},{4,2},{5,3},{6,4},{7,5},{8,14},{9,15},{10,... | collective-permute-start | bytes 1179656 | tf_op jit(solution)/shard_map/reduce/ppermute | solution.py:39
  215.8 9.7 %copy-start.9 = (bf16[1536,128]{1,0:T(8,128)(2,1)S(1)}, bf16[1536,128]{1,0:T(8,128)(2,1)}, u32[]{:S(2)}) copy-start(bf16[1536,128]{1,0:T(8,128)(2,1)} %get-tuple-element.31) | copy-start | bytes 1179652
  216.7 21.3 %collective-permute-start.48 = (bf16[768,128]{1,0:T(8,128)(2,1)S(1)}, bf16[768,128]{1,0:T(8,128)(2,1)S(1)}, u32[]{:S(2)}, u32[]{:S(2)}) collective-permute-start(bf16[768,128]{1,0:T(8,128)(2,1)S(1)} %get-tuple-element.44), channel_id=1, source_target_pairs={{0,8},{1,9},{2,10},{3,11},{4,12},{5,13},{6,14},{7,15},{8,0},{9,1},... | collective-permute-start | bytes 589832 | tf_op jit(solution)/shard_map/reduce/ppermute | solution.py:39
  226.4 11.6 %collective-permute-start.47 = (bf16[768,128]{1,0:T(8,128)(2,1)S(1)}, bf16[768,128]{1,0:T(8,128)(2,1)S(1)}, u32[]{:S(2)}, u32[]{:S(2)}) collective-permute-start(bf16[768,128]{1,0:T(8,128)(2,1)S(1)} %get-tuple-element.46), channel_id=1, source_target_pairs={{0,8},{1,9},{2,10},{3,11},{4,12},{5,13},{6,14},{7,15},{8,0},{9,1},... | collective-permute-start | bytes 589832 | tf_op jit(solution)/shard_map/reduce/ppermute | solution.py:39
  234.5 4.6 %collective-permute-start.46 = (bf16[768,128]{1,0:T(8,128)(2,1)S(1)}, bf16[768,128]{1,0:T(8,128)(2,1)S(1)}, u32[]{:S(2)}, u32[]{:S(2)}) collective-permute-start(bf16[768,128]{1,0:T(8,128)(2,1)S(1)} %get-tuple-element.48), channel_id=1, source_target_pairs={{0,8},{1,9},{2,10},{3,11},{4,12},{5,13},{6,14},{7,15},{8,0},{9,1},... | collective-permute-start | bytes 589832 | tf_op jit(solution)/shard_map/reduce/ppermute | solution.py:39
  (27 other events, 80.0 us)
